TPU v7x, 32 devices: a whole 2x2x4 slice. The times are simulated.
32 devices in a mesh: chan: 4 (over x, core), tile: 8 (over z, y).
Axes of the slice: x: 2, y: 2, z: 4, core: 2. Of those that a mesh axis runs over, the one named last changes fastest.
Arguments:
- voltages: bfloat16 [4, 2, 2048, 2048], P(None, None, 'tile', 'chan'), may hold values from -16 to 16
- rfi_flags: int32 [4], P('chan'), may hold values 0 or 1
- beam_steer_index: int32 [4, 8], P('chan'), may hold values from 0 to 2047
- start_columns: int32 [4, 32], P('chan'), may hold values from 0 to 2047, as said below
Outputs:
- covariance: float32 [4, 2, 2048, 2048], P('chan', None, 'tile')
- weights: float32 [4, 8, 2, 2048], P('chan', None, None, 'tile')
Inputs may be any that keep to these rules, and one draw needn't show every extreme that they name: `start_columns`: the 32 antenna numbers of one channel are distinct.
All inputs are finite; a program needn't handle non-finite values. No bound on the sum of `rfi_flags` on one device may be relied on, other than what follows from the above.
Results may differ from a plain program's by a relative error of at most 0.0003.
Values may be sent and summed in bfloat16 or wider, within the bound.
A program may use at most 128 MiB of HBM per device.

v0:
```python
import math

import jax
import jax.numpy as jnp
from jax import lax
from jax.sharding import PartitionSpec as P

ARRAY_ELEMENTS = 2048
SNAPSHOT_COUNT = 2048
SUB_ITERS = 4
CG_ITERS = 12


diagonal_loading = 0.1
highest = lax.Precision.HIGHEST


def steering_table(beam_entries):
    element_index = jnp.arange(ARRAY_ELEMENTS, dtype=jnp.int32)
    steer_phases = (beam_entries[..., None] * element_index % ARRAY_ELEMENTS).astype(
        jnp.float32
    ) * (2.0 * math.pi / ARRAY_ELEMENTS)
    return jnp.stack([jnp.cos(steer_phases), jnp.sin(steer_phases)], axis=-2)


def orthonormal(vectors):
    dims_in = vectors.shape
    flattened = vectors.reshape(dims_in[:-2] + (dims_in[-2] * dims_in[-1],))
    gram_matrix = jnp.einsum("...kx,...lx->...kl", flattened, flattened, precision=highest)
    factor = jnp.linalg.cholesky(gram_matrix)
    solved = lax.linalg.triangular_solve(factor, flattened, left_side=True, lower=True)
    return solved.reshape(dims_in)


def apply_rows(covariance, vectors):
    upper_half = vectors[..., 0, :]
    lower_half = vectors[..., 1, :]
    stacked = jnp.stack(
        [jnp.stack([upper_half, -lower_half], -2), jnp.stack([lower_half, upper_half], -2)], -3
    )
    return jnp.einsum("...bhpa,...pra->...bhr", stacked, covariance, precision=highest)


def project(vectors, subspace):
    coefficients = jnp.einsum("...bha,...kha->...bk", vectors, subspace, precision=highest)
    return vectors - jnp.einsum("...bk,...kha->...bha", coefficients, subspace, precision=highest)


def shards(voltages, rfi_flags, beam_steer_index, start_columns):
    turned = lax.all_to_all(voltages, "chan", split_axis=0, concat_axis=3, tiled=True)
    tile_total_count = lax.axis_size("tile")
    block_row_set = ARRAY_ELEMENTS // tile_total_count
    first_row = lax.axis_index("tile") * block_row_set
    gathered = lax.all_gather(turned, "tile", axis=2, tiled=True)
    own_rows = lax.dynamic_slice_in_dim(gathered, first_row, block_row_set, 3)
    swapped = jnp.stack([own_rows[:, 1], -own_rows[:, 0]], 1)
    real_part = jnp.einsum("cpsi,cpsj->cij", own_rows, gathered, preferred_element_type=jnp.float32)
    imag_part = jnp.einsum("cpsi,cpsj->cij", swapped, gathered, preferred_element_type=jnp.float32)
    summed = jnp.stack([real_part, imag_part], 1)
    covariance = summed * (1.0 / SNAPSHOT_COUNT)
    diagonal = lax.dynamic_slice_in_dim(covariance[:, 0], first_row, block_row_set, 2)
    covariance_trace = lax.psum(jnp.sum(jnp.diagonal(diagonal, axis1=1, axis2=2), axis=1), "tile")
    loading_amount = diagonal_loading * covariance_trace / ARRAY_ELEMENTS
    picked = jnp.take_along_axis(covariance, start_columns[:, None, None, :], axis=3)
    col_real = jnp.swapaxes(picked[:, 0], 1, 2)
    col_imag = jnp.swapaxes(picked[:, 1], 1, 2)
    rows_now = jnp.concatenate(
        [jnp.stack([col_real, col_imag], 2), jnp.stack([-col_imag, col_real], 2)], 1
    )
    for sweep_index in range(SUB_ITERS):
        full_rows = lax.all_gather(rows_now, "tile", axis=3, tiled=True)
        subspace = orthonormal(full_rows)
        if sweep_index + 1 < SUB_ITERS:
            rows_now = apply_rows(covariance, subspace)
    subspace = subspace * rfi_flags.astype(jnp.float32)[:, None, None, None]
    steering = steering_table(beam_steer_index)
    load_wide = loading_amount[:, None, None, None]
    load_narrow = loading_amount[:, None]

    def cg_sweep(counter, state_tuple):
        solved_weights, residual, direction, res_norm = state_tuple
        projected = project(direction, subspace)
        mapped = lax.all_gather(apply_rows(covariance, projected), "tile", axis=3, tiled=True)
        combined = project(mapped, subspace) + load_wide * direction
        curvature = jnp.sum(projected * mapped, axis=(2, 3)) + load_narrow * jnp.sum(
            direction * direction, axis=(2, 3)
        )
        step_size = res_norm / curvature
        solved_weights = solved_weights + step_size[:, :, None, None] * direction
        residual = residual - step_size[:, :, None, None] * combined
        new_norm = jnp.sum(residual * residual, axis=(2, 3))
        direction = residual + (new_norm / res_norm)[:, :, None, None] * direction
        return (solved_weights, residual, direction, new_norm)

    start_state = (
        jnp.zeros_like(steering),
        steering,
        steering,
        jnp.sum(steering * steering, axis=(2, 3)),
    )
    solved_weights = lax.fori_loop(0, CG_ITERS, cg_sweep, start_state)[0]
    array_response = jnp.sum(steering * solved_weights, axis=(2, 3))
    weights = ARRAY_ELEMENTS * solved_weights / array_response[:, :, None, None]
    shard_local_rows = lax.dynamic_slice_in_dim(weights, first_row, block_row_set, 3)
    return (covariance, shard_local_rows)


def solution(mesh):
    in_specs = (P(None, None, "tile", "chan"), P("chan"), P("chan", None), P("chan", None))
    out_specs = (P("chan", None, "tile", None), P("chan", None, None, "tile"))
    return jax.shard_map(shards, mesh=mesh, in_specs=in_specs, out_specs=out_specs, check_vma=False)
```

profile of v0, /device:TPU:0, one launch (start us, length us, event | category | flops | bytes accessed | tf_op | source)
XLA Modules:
  0.0 1036.3 jit_solution(10615257631190960751)
XLA Ops:
  7.2 29.9 %all_to_all.18 = bf16[4,2,256,512]{3,2,1,0:T(8,128)(2,1)S(1)} all-to-all(bf16[4,2,256,512]{3,2,1,0:T(8,128)(2,1)} %param.9), channel_id=1, replica_groups=mesh['chan'=4,'tile'=8] {'chan'}, dimensions={0} | all-to-all | bytes 4194304 | tf_op jit(solution)/shard_map/all_to_all | solution.py:50
  39.4 228.2 %all-gather.13.cloned.1.call-done = bf16[1,2,2048,2048]{3,2,1,0:T(8,128)(2,1)} async-done(((bf16[1,2,256,2048]{3,2,1,0:T(8,128)(2,1)}), bf16[1,2,2048,2048]{3,2,1,0:T(8,128)(2,1)}) %all-gather.13.cloned.1.call-update) | async-done | bytes 16777232 | tf_op jit(solution)/shard_map/all_gather | solution.py:54
  267.7 8.9 fusion.24
  279.3 4.5 fusion.22
  287.6 7.3 copy.78
  294.9 2.8 gather_fusion
  299.0 37.4 %all-gather.15.cloned.1.call-done = f32[1,64,2,2048]{3,1,2,0:T(8,128)} async-done(((f32[1,64,2,256]{3,1,2,0:T(8,128)}), f32[1,64,2,2048]{3,1,2,0:T(8,128)}) %all-gather.15.cloned.1.call-update) | async-done | bytes 1048592 | tf_op jit(solution)/shard_map/all_gather | solution.py:71
  339.0 5.8 custom-call.15
  346.2 4.9 custom-call.16
  360.6 5.0 fusion.47
  365.9 38.4 %all-gather.17.cloned.1.call-done = f32[64,2,2048]{2,0,1:T(8,128)} async-done(((f32[64,2,256]{2,0,1:T(8,128)}), f32[64,2,2048]{2,0,1:T(8,128)}) %all-gather.17.cloned.1.call-update) | async-done | bytes 1048592 | tf_op jit(solution)/shard_map/all_gather | solution.py:71
  404.2 2.6 fusion.105
  406.9 5.8 custom-call.17
  414.1 4.9 custom-call.18
  426.0 5.0 fusion.50
  431.3 38.3 %all-gather.19.cloned.1.call-done = f32[64,2,2048]{2,0,1:T(8,128)} async-done(((f32[64,2,256]{2,0,1:T(8,128)}), f32[64,2,2048]{2,0,1:T(8,128)}) %all-gather.19.cloned.1.call-update) | async-done | bytes 1048592 | tf_op jit(solution)/shard_map/all_gather | solution.py:71
  472.3 5.8 custom-call.19
  479.5 4.9 custom-call.20
  491.4 5.0 fusion.53
  504.9 20.4 %psum.7 = f32[1]{0:T(128)} all-reduce(f32[1]{0:T(128)} %bitcast.75), channel_id=1, replica_groups=mesh['chan'=4,'tile'=8] {'tile'}, use_global_device_ids=true, to_apply=%region_4.7 | all-reduce | flops 1 | bytes 8 | tf_op jit(solution)/shard_map/psum | solution.py:62
  525.9 9.1 all-gather.21.cloned.1.call-done
  537.7 5.8 custom-call.21
  544.9 4.9 custom-call.22
  551.0 477.3 %while.17 = (s32[]{:T(128)}, f32[1,8,2,2048]{3,1,2,0:T(8,128)S(1)}, f32[1,8,2,2048]{3,1,2,0:T(8,128)S(1)}, f32[1,8,2,2048]{3,1,2,0:T(8,128)S(1)}, f32[1,8]{1,0:T...) while((s32[]{:T(128)}, f32[1,8,2,2048]{3,1,2,0:T(8,128)S(1)}, ...), condition=%wide.region_9.12_spmd.clone, body=%wide.region_5.11_spmd.clone.sunk | while | flops 302694432 | bytes 11706975 | solution.py:101
  552.6 5.5 fusion.146
  558.2 30.5 %all-gather.6 = f32[8,2,2048]{2,0,1:T(8,128)S(1)} all-gather(f32[8,2,256]{2,0,1:T(8,128)S(1)} %fusion.146), channel_id=2, replica_groups=mesh['chan'=4,'tile'=8] {'tile'}, dimensions={2}, use_global_device_ids=true | all-gather | bytes 147456 | tf_op jit(solution)/shard_map/while/body/eval_jaxpr/all_gather | solution.py:83
  592.4 5.5 fusion.146
  597.9 30.5 %all-gather.6 = f32[8,2,2048]{2,0,1:T(8,128)S(1)} all-gather(f32[8,2,256]{2,0,1:T(8,128)S(1)} %fusion.146), channel_id=2, replica_groups=mesh['chan'=4,'tile'=8] {'tile'}, dimensions={2}, use_global_device_ids=true | all-gather | bytes 147456 | tf_op jit(solution)/shard_map/while/body/eval_jaxpr/all_gather | solution.py:83
  632.2 5.5 fusion.146
  637.7 30.5 %all-gather.6 = f32[8,2,2048]{2,0,1:T(8,128)S(1)} all-gather(f32[8,2,256]{2,0,1:T(8,128)S(1)} %fusion.146), channel_id=2, replica_groups=mesh['chan'=4,'tile'=8] {'tile'}, dimensions={2}, use_global_device_ids=true | all-gather | bytes 147456 | tf_op jit(solution)/shard_map/while/body/eval_jaxpr/all_gather | solution.py:83
  672.0 5.5 fusion.146
  677.5 30.5 %all-gather.6 = f32[8,2,2048]{2,0,1:T(8,128)S(1)} all-gather(f32[8,2,256]{2,0,1:T(8,128)S(1)} %fusion.146), channel_id=2, replica_groups=mesh['chan'=4,'tile'=8] {'tile'}, dimensions={2}, use_global_device_ids=true | all-gather | bytes 147456 | tf_op jit(solution)/shard_map/while/body/eval_jaxpr/all_gather | solution.py:83
  711.7 5.5 fusion.146
  717.3 30.5 %all-gather.6 = f32[8,2,2048]{2,0,1:T(8,128)S(1)} all-gather(f32[8,2,256]{2,0,1:T(8,128)S(1)} %fusion.146), channel_id=2, replica_groups=mesh['chan'=4,'tile'=8] {'tile'}, dimensions={2}, use_global_device_ids=true | all-gather | bytes 147456 | tf_op jit(solution)/shard_map/while/body/eval_jaxpr/all_gather | solution.py:83
  751.5 5.5 fusion.146
  757.1 30.5 %all-gather.6 = f32[8,2,2048]{2,0,1:T(8,128)S(1)} all-gather(f32[8,2,256]{2,0,1:T(8,128)S(1)} %fusion.146), channel_id=2, replica_groups=mesh['chan'=4,'tile'=8] {'tile'}, dimensions={2}, use_global_device_ids=true | all-gather | bytes 147456 | tf_op jit(solution)/shard_map/while/body/eval_jaxpr/all_gather | solution.py:83
  791.3 5.5 fusion.146
  796.8 30.5 %all-gather.6 = f32[8,2,2048]{2,0,1:T(8,128)S(1)} all-gather(f32[8,2,256]{2,0,1:T(8,128)S(1)} %fusion.146), channel_id=2, replica_groups=mesh['chan'=4,'tile'=8] {'tile'}, dimensions={2}, use_global_device_ids=true | all-gather | bytes 147456 | tf_op jit(solution)/shard_map/while/body/eval_jaxpr/all_gather | solution.py:83
  831.1 5.5 fusion.146
  836.6 30.5 %all-gather.6 = f32[8,2,2048]{2,0,1:T(8,128)S(1)} all-gather(f32[8,2,256]{2,0,1:T(8,128)S(1)} %fusion.146), channel_id=2, replica_groups=mesh['chan'=4,'tile'=8] {'tile'}, dimensions={2}, use_global_device_ids=true | all-gather | bytes 147456 | tf_op jit(solution)/shard_map/while/body/eval_jaxpr/all_gather | solution.py:83
  870.9 5.5 fusion.146
  876.4 30.5 %all-gather.6 = f32[8,2,2048]{2,0,1:T(8,128)S(1)} all-gather(f32[8,2,256]{2,0,1:T(8,128)S(1)} %fusion.146), channel_id=2, replica_groups=mesh['chan'=4,'tile'=8] {'tile'}, dimensions={2}, use_global_device_ids=true | all-gather | bytes 147456 | tf_op jit(solution)/shard_map/while/body/eval_jaxpr/all_gather | solution.py:83
  910.6 5.5 fusion.146
  916.2 30.5 %all-gather.6 = f32[8,2,2048]{2,0,1:T(8,128)S(1)} all-gather(f32[8,2,256]{2,0,1:T(8,128)S(1)} %fusion.146), channel_id=2, replica_groups=mesh['chan'=4,'tile'=8] {'tile'}, dimensions={2}, use_global_device_ids=true | all-gather | bytes 147456 | tf_op jit(solution)/shard_map/while/body/eval_jaxpr/all_gather | solution.py:83
  950.4 5.5 fusion.146
  955.9 30.5 %all-gather.6 = f32[8,2,2048]{2,0,1:T(8,128)S(1)} all-gather(f32[8,2,256]{2,0,1:T(8,128)S(1)} %fusion.146), channel_id=2, replica_groups=mesh['chan'=4,'tile'=8] {'tile'}, dimensions={2}, use_global_device_ids=true | all-gather | bytes 147456 | tf_op jit(solution)/shard_map/while/body/eval_jaxpr/all_gather | solution.py:83
  990.2 5.5 fusion.146
  995.7 30.5 %all-gather.6 = f32[8,2,2048]{2,0,1:T(8,128)S(1)} all-gather(f32[8,2,256]{2,0,1:T(8,128)S(1)} %fusion.146), channel_id=2, replica_groups=mesh['chan'=4,'tile'=8] {'tile'}, dimensions={2}, use_global_device_ids=true | all-gather | bytes 147456 | tf_op jit(solution)/shard_map/while/body/eval_jaxpr/all_gather | solution.py:83
  (249 shorter events, 101.1 us)
Async XLA Ops:
  7.2 260.5 %all-gather.13.cloned.1.call-start = ((), (), s32[]{:S(2)}) async-start(), calls=%async_computation.1 | async-start | bytes 18874368 | tf_op jit(solution)/shard_map/all_gather | solution.py:54
  38.8 0.7 copy-start.10
  38.8 297.6 %all-gather.15.cloned.1.call-start = ((), (), s32[]{:S(2)}) async-start(), calls=%async_computation.2 | async-start | bytes 1179648 | tf_op jit(solution)/shard_map/all_gather | solution.py:71
  267.7 11.2 %copy-start.1 = (bf16[1,2,2048,2048]{3,2,1,0:T(8,128)(2,1)S(1)}, bf16[1,2,2048,2048]{3,2,1,0:T(8,128)(2,1)}, u32[]{:S(2)}) copy-start(bf16[1,2,2048,2048]{3,2,1,0:T(8,128)(2,1)} %all-gather.13.cloned.1.call-done) | copy-start | bytes 50331652
  283.8 1.3 copy-start.2
  298.5 105.7 %all-gather.17.cloned.1.call-start = ((), (), s32[]{:S(2)}) async-start(), calls=%async_computation.3 | async-start | bytes 1179648 | tf_op jit(solution)/shard_map/all_gather | solution.py:71
  359.0 1.6 copy-start.3
  365.6 103.9 %all-gather.19.cloned.1.call-start = ((), (), s32[]{:S(2)}) async-start(), calls=%async_computation.4 | async-start | bytes 1179648 | tf_op jit(solution)/shard_map/all_gather | solution.py:71
  404.2 14.8 %copy-start.7 = (f32[64,2,2048]{2,0,1:T(8,128)S(1)}, f32[64,2,2048]{2,0,1:T(8,128)}, u32[]{:S(2)}) copy-start(f32[64,2,2048]{2,0,1:T(8,128)} %all-gather.17.cloned.1.call-done) | copy-start | bytes 3145732
  424.4 1.6 copy-start.4
  431.0 104.0 %all-gather.21.cloned.1.call-start = ((), (), s32[]{:S(2)}) async-start(), calls=%async_computation.5 | async-start | bytes 1179648 | tf_op jit(solution)/shard_map/all_gather | solution.py:71
  469.6 14.8 %copy-start.8 = (f32[64,2,2048]{2,0,1:T(8,128)S(1)}, f32[64,2,2048]{2,0,1:T(8,128)}, u32[]{:S(2)}) copy-start(f32[64,2,2048]{2,0,1:T(8,128)} %all-gather.19.cloned.1.call-done) | copy-start | bytes 3145732
  489.8 1.6 copy-start.5
  491.4 5.7 copy-start.9
  499.8 2.0 copy-start
  535.0 14.8 %copy-start.6 = (f32[64,2,2048]{2,0,1:T(8,128)S(1)}, f32[64,2,2048]{2,0,1:T(8,128)}, u32[]{:S(2)}) copy-start(f32[64,2,2048]{2,0,1:T(8,128)} %all-gather.21.cloned.1.call-done) | copy-start | bytes 3145732
Sparse Core Ops, SparseCore 0:
  38.9 228.7 all-gather.12
  298.6 37.7 all-gather.14
  365.8 38.4 all-gather.16
  431.1 38.4 all-gather.18
  496.5 38.4 all-gather.20
where the time goes:
time: 1040 us
  blocking collectives  417 us (40%)
  waiting for transfers between devices  351 us (34%)
  matrix products  150 us (14%)
  other arithmetic  63.1 us (6%)
  local copies, waits for them, and re-layouts  36.8 us (4%)
  between operations  15.9 us (2%)
    all_gather x12, blocking collectives, cg_sweep(): lax.all_gather(apply_rows(covariance, projected), 'tile', axis=3, tiled=T...  366 us
    all_gather x1, waiting for transfers between devices, shards(): gathered = lax.all_gather(turned, 'tile', axis=2, tiled=True)  228 us
    all_gather x4, waiting for transfers between devices, shards(): full_rows = lax.all_gather(rows_now, 'tile', axis=3, tiled=True)  123 us
    dot_general x15, matrix products, apply_rows(): jnp.einsum('...bhpa,...pra->...bhr', stacked, covariance, precision=highest)  81.3 us
    all_to_all x1, blocking collectives, shards(): lax.all_to_all(voltages, 'chan', split_axis=0, concat_axis=3, tiled=True)  29.9 us
    another operation x12, other arithmetic, orthonormal(): factor = jnp.linalg.cholesky(gram_matrix)  26.1 us
    another operation x8, other arithmetic, orthonormal(): lax.linalg.triangular_solve(factor, flattened, left_side=True, lower=True)  22.2 us
    dot_general x24, matrix products, project(): jnp.einsum('...bha,...kha->...bk', vectors, subspace, precision=highest)  22 us
  transfers between devices with their start and end apart: 5, of which 5 were waited for; matrix products, arithmetic and copies ran while one was open for 1% of the time, Pallas kernels for 0%

commit v1 on v0

v1 whole, which is shorter than its diff:
```python
import functools
import math

import jax
import jax.numpy as jnp
from jax import lax
from jax.experimental import pallas as pl
from jax.experimental.pallas import tpu as pltpu
from jax.sharding import PartitionSpec as P

SUB_ITERS = 4
CG_ITERS = 12


diagonal_loading = 0.1
highest = lax.Precision.HIGHEST
MESH = pl.DeviceIdType.MESH


def steering_table(beam_entries, element_total):
    element_index = jnp.arange(element_total, dtype=jnp.int32)
    steer_phases = (beam_entries[..., None] * element_index % element_total).astype(
        jnp.float32
    ) * (2.0 * math.pi / element_total)
    return jnp.stack([jnp.cos(steer_phases), jnp.sin(steer_phases)], axis=0)


def dot_nt(a, b):
    return lax.dot_general(
        a, b, (((1,), (1,)), ((), ())), precision=highest, preferred_element_type=jnp.float32
    )


def dot_nn(a, b):
    return lax.dot_general(
        a, b, (((1,), (0,)), ((), ())), precision=highest, preferred_element_type=jnp.float32
    )


def dot_nt16(a, b):
    return lax.dot_general(a, b, (((1,), (1,)), ((), ())), preferred_element_type=jnp.float32)


def split_halves(values):
    high = values.astype(jnp.bfloat16)
    low = (values - high.astype(jnp.float32)).astype(jnp.bfloat16)
    return high, low


def complex_rows(product, count, rows):
    real = product[:count, :rows] - product[count:, rows:]
    imag = product[count:, :rows] + product[:count, rows:]
    return jnp.concatenate([real, imag], 0)


def embed(real, imag):
    return jnp.concatenate(
        [jnp.concatenate([real, -imag], 1), jnp.concatenate([imag, real], 1)], 0
    )


def hermitian_parts(product, count):
    real = product[:count, :count] + product[count:, count:]
    imag = product[count:, :count] - product[:count, count:]
    return real, imag


def inverse_factor(gram_real, gram_imag, count):
    row_id = lax.broadcasted_iota(jnp.int32, (count, count), 0)
    col_id = lax.broadcasted_iota(jnp.int32, (count, count), 1)
    eye = (row_id == col_id).astype(jnp.float32)
    system = jnp.concatenate([gram_real, gram_imag, eye, jnp.zeros_like(eye)], 1)
    below = lax.broadcasted_iota(jnp.int32, (count, 1), 0)
    lane = lax.broadcasted_iota(jnp.int32, (1, 4 * count), 1)
    first_half = lax.rem(lane, 2 * count) < count
    for k in range(count):
        row = system[k : k + 1, :]
        fore = pltpu.roll(row, 3 * count, 1)
        back = pltpu.roll(row, count, 1)
        turned = jnp.where(first_half, -fore, back)
        scale = jnp.where(below > k, 1.0 / row[:, k : k + 1], 0.0)
        factor_real = system[:, k : k + 1] * scale
        factor_imag = system[:, count + k : count + k + 1] * scale
        system = system - factor_real * row - factor_imag * turned
    pivots = jnp.sum(system[:, :count] * eye, axis=1, keepdims=True)
    system = system * lax.rsqrt(pivots)
    return embed(system[:, 2 * count : 3 * count], system[:, 3 * count :])


def tail_kernel(
    peers,
    cov_ref,
    columns_ref,
    flag_ref,
    steer_ref,
    out_ref,
    vectors,
    mapped,
    traces,
    factor_ref,
    basis_ref,
    wide_ref,
    high_ref,
    low_ref,
    x_ref,
    r_ref,
    p_ref,
    vec_send,
    vec_recv,
    map_send,
    map_recv,
    tr_send,
    tr_recv,
):
    me = lax.axis_index("tile")
    rows = cov_ref.shape[0] // 2
    antennas = cov_ref.shape[1]
    count = columns_ref.shape[1]
    beams = steer_ref.shape[0] // 2
    own = pl.ds(pl.multiple_of(me * rows, rows), rows)

    barrier = pltpu.get_barrier_semaphore()
    for k in range(1, peers):
        pl.semaphore_signal(
            barrier, inc=1, device_id={"tile": lax.rem(me + k, peers)}, device_id_type=MESH
        )
    pl.semaphore_wait(barrier, peers - 1)

    def send(block, send_sem, recv_sem):
        for k in range(1, peers):
            pltpu.make_async_remote_copy(
                src_ref=block.at[me],
                dst_ref=block.at[me],
                send_sem=send_sem.at[k],
                recv_sem=recv_sem.at[k],
                device_id={"tile": lax.rem(me + k, peers)},
                device_id_type=MESH,
            ).start()

    def arrive(block, send_sem, recv_sem):
        for k in range(1, peers):
            source = lax.rem(me - k + peers, peers)
            copy = pltpu.make_async_remote_copy(
                src_ref=block.at[me],
                dst_ref=block.at[source],
                send_sem=send_sem.at[k],
                recv_sem=recv_sem.at[k],
                device_id={"tile": lax.rem(me + k, peers)},
                device_id_type=MESH,
            )
            copy.wait_send()
            copy.wait_recv()

    def whole(block):
        return jnp.concatenate([block[j] for j in range(peers)], 1)

    hot = (
        lax.broadcasted_iota(jnp.int32, (antennas, count), 0) == columns_ref[0:1, :]
    ).astype(jnp.float32)
    picked = lax.dot_general(
        hot, cov_ref[...], (((0,), (1,)), ((), ())), precision=highest,
        preferred_element_type=jnp.float32,
    )
    vectors[0, me] = jnp.concatenate([picked[:, :rows], picked[:, rows:]], 0)
    send(vectors.at[0], vec_send.at[0], vec_recv.at[0])

    square = cov_ref[0:rows, own]
    on_diagonal = lax.broadcasted_iota(jnp.int32, (rows, rows), 0) == lax.broadcasted_iota(
        jnp.int32, (rows, rows), 1
    )
    own_trace = jnp.sum(jnp.where(on_diagonal, square, 0.0), axis=(0, 1), keepdims=True)
    traces[me] = jnp.broadcast_to(own_trace, traces.shape[1:])
    send(traces, tr_send, tr_recv)

    def subspace_round(step, carry):
        now, later = lax.rem(step, 2), lax.rem(step + 1, 2)
        arrive(vectors.at[now], vec_send.at[now], vec_recv.at[now])
        block = whole(vectors.at[now])
        moved = complex_rows(dot_nt(block, cov_ref[...]), count, rows)
        factor = inverse_factor(*hermitian_parts(dot_nt(block, block), count), count)
        factor_ref[...] = factor
        vectors[later, me] = dot_nn(factor, moved)
        send(vectors.at[later], vec_send.at[later], vec_recv.at[later])
        return carry

    lax.fori_loop(0, SUB_ITERS, subspace_round, 0)
    last, after = (SUB_ITERS - 1) % 2, SUB_ITERS % 2
    flag = flag_ref[...].astype(jnp.float32)
    basis = dot_nn(factor_ref[...], whole(vectors.at[last])) * flag
    basis_ref[...] = basis
    arrive(vectors.at[after], vec_send.at[after], vec_recv.at[after])
    image = whole(vectors.at[after]) * flag
    inner = embed(*hermitian_parts(dot_nt(image, basis), count))
    wide_ref[0 : 2 * count, :] = image - 0.5 * dot_nn(inner, basis)
    wide_ref[2 * count :, :] = basis
    own_basis = basis_ref[:, own]
    own_wide = wide_ref[0 : 2 * count, own]
    left_real = jnp.concatenate([own_basis, own_wide], 0)
    left_imag = jnp.concatenate(
        [own_basis[count:], -own_basis[:count], own_wide[count:], -own_wide[:count]], 0
    )
    left = jnp.concatenate([left_real.T, left_imag.T], 0)

    @pl.loop(0, peers)
    def _(j):
        part = pl.ds(pl.multiple_of(j * rows, rows), rows)
        projected = cov_ref[:, part] - dot_nn(left, wide_ref[:, part])
        high, low = split_halves(projected)
        high_ref[:, part] = high
        low_ref[:, part] = low

    arrive(traces, tr_send, tr_recv)
    trace = traces[0, 0:1, 0:1]
    for j in range(1, peers):
        trace = trace + traces[j, 0:1, 0:1]
    load = diagonal_loading * trace / antennas

    def inner_product(a, b):
        each = jnp.sum(a * b, axis=1, keepdims=True)
        return each[:beams] + each[beams:]

    def both(each):
        return jnp.concatenate([each, each], 0)

    steering = steer_ref[...]
    x_ref[...] = jnp.zeros_like(steering)
    r_ref[...] = steering
    p_ref[...] = steering

    def cg_step(step, norm):
        slot = lax.rem(step, 2)
        direction = p_ref[...]
        high, low = split_halves(direction)
        top = dot_nt16(jnp.concatenate([high, low], 0), high_ref[...])
        product = top[: 2 * beams] + top[2 * beams :] + dot_nt16(high, low_ref[...])
        mapped[slot, me] = complex_rows(product, beams, rows)
        send(mapped.at[slot], map_send.at[slot], map_recv.at[slot])
        arrive(mapped.at[slot], map_send.at[slot], map_recv.at[slot])
        combined = whole(mapped.at[slot]) + load * direction
        alpha = norm / inner_product(direction, combined)
        alpha_rows = both(alpha)
        x_ref[...] = x_ref[...] + alpha_rows * direction
        residual = r_ref[...] - alpha_rows * combined
        r_ref[...] = residual
        new_norm = inner_product(residual, residual)
        p_ref[...] = residual + both(new_norm / norm) * direction
        return new_norm

    lax.fori_loop(0, CG_ITERS, cg_step, inner_product(steering, steering))
    response = both(inner_product(steer_ref[...], x_ref[...]))
    out_ref[...] = antennas * x_ref[:, own] / response


def beam_weights(covariance, rfi_flags, beam_steer_index, start_columns):
    peers = lax.axis_size("tile")
    _, _, rows, antennas = covariance.shape
    beams = beam_steer_index.shape[1]
    count = start_columns.shape[1]
    steering = steering_table(beam_steer_index[0], antennas).reshape(2 * beams, antennas)
    f32, b16 = jnp.float32, jnp.bfloat16
    dma = pltpu.SemaphoreType.DMA
    out = pl.pallas_call(
        functools.partial(tail_kernel, peers),
        out_shape=jax.ShapeDtypeStruct((2 * beams, rows), f32),
        in_specs=[pl.BlockSpec(memory_space=pltpu.VMEM)] * 4,
        out_specs=pl.BlockSpec(memory_space=pltpu.VMEM),
        scratch_shapes=[
            pltpu.VMEM((2, peers, 2 * count, rows), f32),
            pltpu.VMEM((2, peers, 2 * beams, rows), f32),
            pltpu.VMEM((peers, 8, 128), f32),
            pltpu.VMEM((2 * count, 2 * count), f32),
            pltpu.VMEM((2 * count, antennas), f32),
            pltpu.VMEM((4 * count, antennas), f32),
            pltpu.VMEM((2 * rows, antennas), b16),
            pltpu.VMEM((2 * rows, antennas), b16),
            pltpu.VMEM((2 * beams, antennas), f32),
            pltpu.VMEM((2 * beams, antennas), f32),
            pltpu.VMEM((2 * beams, antennas), f32),
            dma((2, peers)),
            dma((2, peers)),
            dma((2, peers)),
            dma((2, peers)),
            dma((peers,)),
            dma((peers,)),
        ],
        compiler_params=pltpu.CompilerParams(
            collective_id=0, has_side_effects=True, vmem_limit_bytes=48 * 1024 * 1024
        ),
    )(
        covariance.reshape(2 * rows, antennas),
        start_columns,
        rfi_flags.reshape(1, 1),
        steering,
    )
    return jnp.swapaxes(out.reshape(2, beams, rows), 0, 1)[None]


def shards(voltages, rfi_flags, beam_steer_index, start_columns):
    turned = lax.all_to_all(voltages, "chan", split_axis=0, concat_axis=3, tiled=True)
    snapshots = voltages.shape[2] * lax.axis_size("tile")
    rows = turned.shape[3] // lax.axis_size("tile")
    first_row = lax.axis_index("tile") * rows
    gathered = lax.all_gather(turned, "tile", axis=2, tiled=True)
    own_rows = lax.dynamic_slice_in_dim(gathered, first_row, rows, 3)
    swapped = jnp.stack([own_rows[:, 1], -own_rows[:, 0]], 1)
    real_part = jnp.einsum("cpsi,cpsj->cij", own_rows, gathered, preferred_element_type=jnp.float32)
    imag_part = jnp.einsum("cpsi,cpsj->cij", swapped, gathered, preferred_element_type=jnp.float32)
    covariance = jnp.stack([real_part, imag_part], 1) * (1.0 / snapshots)
    weights = beam_weights(covariance, rfi_flags, beam_steer_index, start_columns)
    return (covariance, weights)


def solution(mesh):
    in_specs = (P(None, None, "tile", "chan"), P("chan"), P("chan", None), P("chan", None))
    out_specs = (P("chan", None, "tile", None), P("chan", None, None, "tile"))
    return jax.shard_map(shards, mesh=mesh, in_specs=in_specs, out_specs=out_specs, check_vma=False)
```

time: 1040 us -> 477 us (0.46)
  blocking collectives: 417 us -> 29.9 us
  Pallas kernels: 0 us -> 185 us
  matrix products: 150 us -> 13.5 us
  waiting for transfers between devices: 351 us -> 228 us
  other arithmetic: 63.1 us -> 1.13 us
  local copies, waits for them, and re-layouts: 36.8 us -> 4.79 us
    all_gather x12 -> x0, blocking collectives: 366 us -> none  [cg_sweep(): lax.all_gather(apply_rows(covariance, projected), 'tile', axis=3, tiled=T...]
    pallas_call x0 -> x1, Pallas kernels: none -> 185 us  [beam_weights(): pl.pallas_call(functools.partial(tail_kernel, peers), out_shape=jax.Shape...]
    dot_general x67 -> x0, matrix products: 130 us -> none  [the longest x15 81.3 us: apply_rows(): jnp.einsum('...bhpa,...pra->...bhr', stacked, covariance, precision=highest)]
    all_gather x4 -> x0, waiting for transfers between devices: 123 us -> none  [shards(): full_rows = lax.all_gather(rows_now, 'tile', axis=3, tiled=True)]
    another operation x38 -> x0, other arithmetic: 49.7 us -> none  [the longest x12 26.1 us: orthonormal(): factor = jnp.linalg.cholesky(gram_matrix)]
    psum x1 -> x0, blocking collectives: 20.4 us -> none  [shards(): lax.psum(jnp.sum(jnp.diagonal(diagonal, axis1=1, axis2=2), axis=1), 'tile')]
  transfers between devices with their start and end apart: 5 -> 1, of which waited for: 5 -> 1; matrix products, arithmetic and copies ran while one was open for 1% -> 0% of each run, Pallas kernels for 0% -> 0%
where the time goes in v1:
time: 477 us
  waiting for transfers between devices  228 us (48%)
  Pallas kernels  185 us (39%)
  blocking collectives  29.9 us (6%)
  between operations  14.8 us (3%)
  matrix products  13.5 us (3%)
  local copies, waits for them, and re-layouts  4.79 us (1%)
    all_gather x1, waiting for transfers between devices, shards(): gathered = lax.all_gather(turned, 'tile', axis=2, tiled=True)  228 us
    pallas_call x1, Pallas kernels, beam_weights(): pl.pallas_call(functools.partial(tail_kernel, peers), out_shape=jax.Shape...  185 us
    all_to_all x1, blocking collectives, shards(): lax.all_to_all(voltages, 'chan', split_axis=0, concat_axis=3, tiled=True)  29.9 us
  transfers between devices with their start and end apart: 1, of which 1 were waited for; matrix products, arithmetic and copies ran while one was open for 0% of the time, Pallas kernels for 0%

profile of v1, /device:TPU:0, one launch (start us, length us, event | category | flops | bytes accessed | tf_op | source)
XLA Modules:
  0.0 476.7 jit_solution(12721679897308245916)
XLA Ops:
  7.2 0.0 all-gather.2.cloned.1.call-start
  7.2 29.9 %all_to_all.18 = bf16[4,2,256,512]{3,2,1,0:T(8,128)(2,1)S(1)} all-to-all(bf16[4,2,256,512]{3,2,1,0:T(8,128)(2,1)} %param.4), channel_id=1, replica_groups=mesh['chan'=4,'tile'=8] {'chan'}, dimensions={0} | all-to-all | bytes 4194304 | tf_op jit(solution)/shard_map/all_to_all | solution.py:299
  37.1 1.6 copy.15
  38.8 0.0 copy-start.3
  38.8 0.0 all-gather.2.cloned.1.call-update
  39.4 0.0 copy-done.3
  39.4 0.3 fusion.21
  39.8 227.9 %all-gather.2.cloned.1.call-done = bf16[1,2,2048,2048]{3,2,1,0:T(8,128)(2,1)} async-done(((bf16[1,2,256,2048]{3,2,1,0:T(8,128)(2,1)}), bf16[1,2,2048,2048]{3,2,1,0:T(8,128)(2,1)}) %all-gather.2.cloned.1.call-update) | async-done | bytes 16777232 | tf_op jit(solution)/shard_map/all_gather | solution.py:303
  267.7 0.0 copy-start.2
  267.7 8.9 %fusion.4 = f32[1,1,256,2048]{3,2,1,0:T(8,128)S(1)} fusion(bf16[1,2,2048,2048]{3,2,1,0:T(8,128)(2,1)} %all-gather.2.cloned.1.call-done, s32[]{:T(128)S(6)} %select_n.21), kind=kOutput, calls=%fused_computation.5 | convolution fusion | flops 4294967296 | bytes 20971524 | tf_op jit(solution)/shard_map/cpsi,cpsj->cij/dot_general | solution.py:306
  276.6 2.2 copy-done.2
  278.8 0.4 constant_dynamic-slice_fusion
  279.3 4.5 fusion.7
  283.8 0.0 copy-start.1
  283.8 0.3 maximum_multiply_fusion
  284.2 0.0 copy-start
  284.2 0.3 copy-done.1
  284.5 184.7 %shard_map.62 = f32[16,256]{1,0:T(8,128)S(1)} custom-call(f32[512,2048]{1,0:T(8,128)S(1)} %bitcast.40, s32[1,32]{1,0:T(1,128)S(1)} %copy-done.1, s32[1,1]{1,0:T(1,128)} %bitcast.39.flag_ref, f32[16,2048]{1,0:T(8,128)S(1)} %maximum_bitcast_fusion.2.steer_ref), custom_call_target="tpu_custom_call" | custom-call | tf_op jit(solution)/shard_map/pallas_call | solution.py:262
  469.2 0.0 copy-done
  469.2 0.6 copy.17
  (1 shorter events, 0.0 us)
Async XLA Ops:
  7.2 260.5 %all-gather.2.cloned.1.call-start = ((), (), s32[]{:S(2)}) async-start(), calls=%async_computation.1 | async-start | bytes 18874368 | tf_op jit(solution)/shard_map/all_gather | solution.py:303
  38.8 0.7 copy-start.3
  267.7 11.2 %copy-start.2 = (bf16[1,2,2048,2048]{3,2,1,0:T(8,128)(2,1)S(1)}, bf16[1,2,2048,2048]{3,2,1,0:T(8,128)(2,1)}, u32[]{:S(2)}) copy-start(bf16[1,2,2048,2048]{3,2,1,0:T(8,128)(2,1)} %all-gather.2.cloned.1.call-done) | copy-start | bytes 50331652
  283.8 0.7 copy-start.1
  284.2 185.1 %copy-start = (f32[1,2,256,2048]{3,2,1,0:T(8,128)}, f32[1,2,256,2048]{3,2,1,0:T(8,128)S(1)}, u32[]{:S(2)}) copy-start(f32[1,2,256,2048]{3,2,1,0:T(8,128)S(1)} %maximum_multiply_fusion) | copy-start | bytes 12582916
Sparse Core Ops, SparseCore 0:
  38.9 228.7 all-gather.1

commit v2 on v1

--- a/solution.py
+++ b/solution.py
@@ -85,6 +85,158 @@
     pivots = jnp.sum(system[:, :count] * eye, axis=1, keepdims=True)
     system = system * lax.rsqrt(pivots)
     return embed(system[:, 2 * count : 3 * count], system[:, 3 * count :])
+
+
+def ring_place(position, peers):
+    half = peers // 2
+    return jnp.where(position < half, 2 * position, 2 * (peers - 1 - position) + 1)
+
+
+def covariance_kernel(
+    peers, groups, volt_ref, cov_ref, shards_ref, left_ref, local_sem, turn_send, turn_recv, ring_send, ring_recv
+):
+    me = lax.axis_index("tile")
+    chan = lax.axis_index("chan")
+    _, _, depth, width = volt_ref.shape
+    rows = cov_ref.shape[0] // 2
+    antennas = cov_ref.shape[1]
+    half = peers // 2
+    own = pl.ds(pl.multiple_of(me * rows, rows), rows)
+    odd = lax.rem(me, 2)
+    position = jnp.where(odd == 0, me // 2, peers - 1 - me // 2)
+
+    def tile_at(offset):
+        return ring_place(lax.rem(position + offset + peers, peers), peers)
+
+    right, left = tile_at(1), tile_at(-1)
+
+    barrier = pltpu.get_barrier_semaphore()
+    for k in range(1, groups):
+        pl.semaphore_signal(
+            barrier, inc=1, device_id={"chan": lax.rem(chan + k, groups)}, device_id_type=MESH
+        )
+    for neighbour in (left, right):
+        pl.semaphore_signal(barrier, inc=1, device_id={"tile": neighbour}, device_id_type=MESH)
+    pl.semaphore_wait(barrier, groups + 1)
+
+    def piece(tile, source):
+        lanes = pl.ds(pl.multiple_of(source * width, width), width)
+        return shards_ref.at[tile, :, :, lanes]
+
+    def turn_copy(k):
+        return pltpu.make_async_remote_copy(
+            src_ref=volt_ref.at[lax.rem(chan + k, groups)],
+            dst_ref=piece(me, chan),
+            send_sem=turn_send.at[k],
+            recv_sem=turn_recv.at[k],
+            device_id={"chan": lax.rem(chan + k, groups)},
+            device_id_type=MESH,
+        )
+
+    def turn_arrival(k):
+        source = lax.rem(chan - k + groups, groups)
+        return pltpu.make_async_remote_copy(
+            src_ref=volt_ref.at[chan],
+            dst_ref=piece(me, source),
+            send_sem=turn_send.at[k],
+            recv_sem=turn_recv.at[k],
+            device_id={"chan": lax.rem(chan + k, groups)},
+            device_id_type=MESH,
+        )
+
+    def hops(way, k):
+        longer = 0 if k < groups // 2 else 1
+        return half if way == longer else half - 1
+
+    def ring_copy(way, hop, k, arriving=False):
+        step = 1 if way == 0 else -1
+        tile = tile_at(-step * (hop + 1 if arriving else hop))
+        part = piece(tile, lax.rem(chan - k + groups, groups))
+        return pltpu.make_async_remote_copy(
+            src_ref=part,
+            dst_ref=part,
+            send_sem=ring_send.at[way, hop, k],
+            recv_sem=ring_recv.at[way, hop, k],
+            device_id={"tile": right if way == 0 else left},
+            device_id_type=MESH,
+        )
+
+    def add_shard(tile, first=False, scale=None):
+        real, imag = shards_ref[tile, 0, :, own], shards_ref[tile, 1, :, own]
+        left_ref[...] = jnp.concatenate(
+            [jnp.concatenate([real, imag], 1), jnp.concatenate([imag, -real], 1)], 0
+        ).T
+
+        @pl.loop(0, peers)
+        def _(j):
+            part = pl.ds(pl.multiple_of(j * rows, rows), rows)
+            right_part = jnp.concatenate(
+                [shards_ref[tile, 0, :, part], shards_ref[tile, 1, :, part]], 0
+            )
+            term = jnp.dot(left_ref[...], right_part, preferred_element_type=jnp.float32)
+            if not first:
+                term = term + cov_ref[:, part]
+            if scale is not None:
+                term = term * scale
+            cov_ref[:, part] = term
+
+    local = pltpu.make_async_copy(volt_ref.at[chan], piece(me, chan), local_sem)
+    for k in range(1, groups):
+        turn_copy(k).start()
+    local.start()
+    for k in range(groups):
+        if k == 0:
+            local.wait()
+        else:
+            turn_arrival(k).wait_recv()
+        for way in range(2):
+            ring_copy(way, 0, k).start()
+    add_shard(me, first=True)
+    for hop in range(half):
+        for k in range(groups):
+            for way in range(2):
+                if hop < hops(way, k):
+                    ring_copy(way, hop, k, arriving=True).wait_recv()
+                    if hop + 1 < hops(way, k):
+                        ring_copy(way, hop + 1, k).start()
+        if hop + 1 < half:
+            add_shard(tile_at(-hop - 1))
+            add_shard(tile_at(hop + 1))
+        else:
+            add_shard(tile_at(half), scale=1.0 / (depth * peers))
+    for k in range(1, groups):
+        turn_copy(k).wait_send()
+    for k in range(groups):
+        for way in range(2):
+            for hop in range(hops(way, k)):
+                ring_copy(way, hop, k).wait_send()
+
+
+def channel_covariance(voltages):
+    peers, groups = lax.axis_size("tile"), lax.axis_size("chan")
+    _, _, depth, width = voltages.shape
+    antennas = width * groups
+    rows = antennas // peers
+    dma = pltpu.SemaphoreType.DMA
+    out = pl.pallas_call(
+        functools.partial(covariance_kernel, peers, groups),
+        out_shape=jax.ShapeDtypeStruct((2 * rows, antennas), jnp.float32),
+        in_specs=[pl.BlockSpec(memory_space=pl.ANY)],
+        out_specs=pl.BlockSpec(memory_space=pltpu.VMEM),
+        scratch_shapes=[
+            pltpu.VMEM((peers, 2, depth, antennas), voltages.dtype),
+            pltpu.VMEM((2 * rows, 2 * depth), voltages.dtype),
+            dma(()),
+            dma((groups,)),
+            dma((groups,)),
+            dma((2, peers // 2, groups)),
+            dma((2, peers // 2, groups)),
+        ],
+        compiler_params=pltpu.CompilerParams(
+            collective_id=1, has_side_effects=True, vmem_limit_bytes=40 * 1024 * 1024
+        ),
+    )(voltages)
+    return out.reshape(1, 2, rows, antennas)
 
 
 def tail_kernel(
@@ -296,16 +448,7 @@
 
 
 def shards(voltages, rfi_flags, beam_steer_index, start_columns):
-    turned = lax.all_to_all(voltages, "chan", split_axis=0, concat_axis=3, tiled=True)
-    snapshots = voltages.shape[2] * lax.axis_size("tile")
-    rows = turned.shape[3] // lax.axis_size("tile")
-    first_row = lax.axis_index("tile") * rows
-    gathered = lax.all_gather(turned, "tile", axis=2, tiled=True)
-    own_rows = lax.dynamic_slice_in_dim(gathered, first_row, rows, 3)
-    swapped = jnp.stack([own_rows[:, 1], -own_rows[:, 0]], 1)
-    real_part = jnp.einsum("cpsi,cpsj->cij", own_rows, gathered, preferred_element_type=jnp.float32)
-    imag_part = jnp.einsum("cpsi,cpsj->cij", swapped, gathered, preferred_element_type=jnp.float32)
-    covariance = jnp.stack([real_part, imag_part], 1) * (1.0 / snapshots)
+    covariance = channel_covariance(voltages)
     weights = beam_weights(covariance, rfi_flags, beam_steer_index, start_columns)
     return (covariance, weights)
 

time: 477 us -> 362 us (0.76)
  waiting for transfers between devices: 228 us -> 0 us
  Pallas kernels: 185 us -> 355 us
  blocking collectives: 29.9 us -> 0 us
  matrix products: 13.5 us -> 0 us
  between operations: 14.8 us -> 1.34 us
    all_gather x1 -> x0, waiting for transfers between devices: 228 us -> none  [shards(): gathered = lax.all_gather(turned, 'tile', axis=2, tiled=True)]
    pallas_call x0 -> x1, Pallas kernels: none -> 165 us  [channel_covariance(): pl.pallas_call(functools.partial(covariance_kernel, peers, groups), out_s...]
    all_to_all x1 -> x0, blocking collectives: 29.9 us -> none  [shards(): lax.all_to_all(voltages, 'chan', split_axis=0, concat_axis=3, tiled=True)]
    dot_general x2 -> x0, matrix products: 13.5 us -> none  [the longest x1 8.9 us: shards(): jnp.einsum('cpsi,cpsj->cij', own_rows, gathered, preferred_element_type=j...]
    pallas_call x1, Pallas kernels: 185 us -> 190 us  [beam_weights(): pl.pallas_call(functools.partial(tail_kernel, peers), out_shape=jax.Shape...]
  transfers between devices with their start and end apart: 1 -> 0, of which waited for: 1 -> 0; matrix products, arithmetic and copies ran while one was open for 0% -> 0% of each run, Pallas kernels for 0% -> 0%
where the time goes in v2:
time: 362 us
  Pallas kernels  355 us (98%)
  local copies, waits for them, and re-layouts  4.22 us (1%)
    pallas_call x1, Pallas kernels, beam_weights(): pl.pallas_call(functools.partial(tail_kernel, peers), out_shape=jax.Shape...  190 us
    pallas_call x1, Pallas kernels, channel_covariance(): pl.pallas_call(functools.partial(covariance_kernel, peers, groups), out_s...  165 us

profile of v2, /device:TPU:0, one launch (start us, length us, event | category | flops | bytes accessed | tf_op | source)
XLA Modules:
  0.0 361.8 jit_solution(11978037279728604978)
XLA Ops:
  0.6 0.0 copy-start.1
  1.3 1.0 fusion.7
  2.3 0.0 copy-start
  2.3 1.6 copy-done
  3.9 165.4 %shard_map.62.cov_ref = f32[512,2048]{1,0:T(8,128)S(1)} custom-call(bf16[4,2,256,512]{3,2,1,0:T(8,128)(2,1)S(1)} %copy-done), custom_call_target="tpu_custom_call" | custom-call | tf_op jit(solution)/shard_map/pallas_call | solution.py:221
  169.4 0.0 copy-done.1
  169.4 189.8 %shard_map.63 = f32[16,256]{1,0:T(8,128)S(1)} custom-call(f32[512,2048]{1,0:T(8,128)S(1)} %shard_map.62.cov_ref, s32[1,32]{1,0:T(1,128)S(1)} %copy-done.1, s32[1,1]{1,0:T(1,128)} %bitcast.11.flag_ref, f32[16,2048]{1,0:T(8,128)S(1)} %maximum_bitcast_fusion.steer_ref), custom_call_target="tpu_custom_call" | custom-call | tf_op jit(solution)/shard_map/pallas_call | solution.py:414
  359.2 0.6 copy.8
  359.8 2.0 copy.11
  (1 shorter events, 0.0 us)
Async XLA Ops:
  0.6 168.7 %copy-start.1 = (s32[1,32]{1,0:T(1,128)S(1)}, s32[1,32]{1,0:T(1,128)}, u32[]{:S(2)}) copy-start(s32[1,32]{1,0:T(1,128)} %columns_ref.1) | copy-start | bytes 388
  2.3 1.6 copy-start

commit v3 on v2

--- a/solution.py
+++ b/solution.py
@@ -37,8 +37,16 @@
     )
 
 
-def dot_nt16(a, b):
-    return lax.dot_general(a, b, (((1,), (1,)), ((), ())), preferred_element_type=jnp.float32)
+def dot16(a, b):
+    return jnp.dot(a, b, preferred_element_type=jnp.float32)
+
+
+def split_thirds(values):
+    high = values.astype(jnp.bfloat16)
+    rest = values - high.astype(jnp.float32)
+    middle = rest.astype(jnp.bfloat16)
+    low = (rest - middle.astype(jnp.float32)).astype(jnp.bfloat16)
+    return high, middle, low
 
 
 def split_halves(values):
@@ -252,8 +260,7 @@
     factor_ref,
     basis_ref,
     wide_ref,
-    high_ref,
-    low_ref,
+    parts_ref,
     x_ref,
     r_ref,
     p_ref,
@@ -267,7 +274,7 @@
     me = lax.axis_index("tile")
     rows = cov_ref.shape[0] // 2
     antennas = cov_ref.shape[1]
-    count = columns_ref.shape[1]
+    count = columns_ref.shape[0]
     beams = steer_ref.shape[0] // 2
     own = pl.ds(pl.multiple_of(me * rows, rows), rows)
 
@@ -306,13 +313,17 @@
     def whole(block):
         return jnp.concatenate([block[j] for j in range(peers)], 1)
 
-    hot = (
-        lax.broadcasted_iota(jnp.int32, (antennas, count), 0) == columns_ref[0:1, :]
-    ).astype(jnp.float32)
-    picked = lax.dot_general(
-        hot, cov_ref[...], (((0,), (1,)), ((), ())), precision=highest,
-        preferred_element_type=jnp.float32,
-    )
+    @pl.loop(0, peers)
+    def _(j):
+        part = pl.ds(pl.multiple_of(j * rows, rows), rows)
+        thirds = split_thirds(cov_ref[:, part].T)
+        for third, values in enumerate(thirds):
+            parts_ref[third, part, :] = values
+
+    hot = jnp.where(
+        lax.broadcasted_iota(jnp.int32, (count, antennas), 1) == columns_ref[...], 1.0, 0.0
+    ).astype(jnp.bfloat16)
+    picked = dot16(hot, parts_ref[0]) + (dot16(hot, parts_ref[1]) + dot16(hot, parts_ref[2]))
     vectors[0, me] = jnp.concatenate([picked[:, :rows], picked[:, rows:]], 0)
     send(vectors.at[0], vec_send.at[0], vec_recv.at[0])
 
@@ -328,7 +339,12 @@
         now, later = lax.rem(step, 2), lax.rem(step + 1, 2)
         arrive(vectors.at[now], vec_send.at[now], vec_recv.at[now])
         block = whole(vectors.at[now])
-        moved = complex_rows(dot_nt(block, cov_ref[...]), count, rows)
+        size = 2 * count
+        high, middle, low = split_thirds(block)
+        top = dot16(jnp.concatenate([high, middle, low], 0), parts_ref[0])
+        mid = dot16(jnp.concatenate([high, middle], 0), parts_ref[1])
+        small = top[2 * size :] + mid[size:] + dot16(high, parts_ref[2])
+        moved = complex_rows(top[:size] + (top[size : 2 * size] + mid[:size] + small), count, rows)
         factor = inverse_factor(*hermitian_parts(dot_nt(block, block), count), count)
         factor_ref[...] = factor
         vectors[later, me] = dot_nn(factor, moved)
@@ -357,9 +373,9 @@
     def _(j):
         part = pl.ds(pl.multiple_of(j * rows, rows), rows)
         projected = cov_ref[:, part] - dot_nn(left, wide_ref[:, part])
-        high, low = split_halves(projected)
-        high_ref[:, part] = high
-        low_ref[:, part] = low
+        high, low = split_halves(projected.T)
+        parts_ref[0, part, :] = high
+        parts_ref[1, part, :] = low
 
     arrive(traces, tr_send, tr_recv)
     trace = traces[0, 0:1, 0:1]
@@ -383,8 +399,8 @@
         slot = lax.rem(step, 2)
         direction = p_ref[...]
         high, low = split_halves(direction)
-        top = dot_nt16(jnp.concatenate([high, low], 0), high_ref[...])
-        product = top[: 2 * beams] + top[2 * beams :] + dot_nt16(high, low_ref[...])
+        top = dot16(jnp.concatenate([high, low], 0), parts_ref[0])
+        product = top[: 2 * beams] + top[2 * beams :] + dot16(high, parts_ref[1])
         mapped[slot, me] = complex_rows(product, beams, rows)
         send(mapped.at[slot], map_send.at[slot], map_recv.at[slot])
         arrive(mapped.at[slot], map_send.at[slot], map_recv.at[slot])
@@ -423,8 +439,7 @@
             pltpu.VMEM((2 * count, 2 * count), f32),
             pltpu.VMEM((2 * count, antennas), f32),
             pltpu.VMEM((4 * count, antennas), f32),
-            pltpu.VMEM((2 * rows, antennas), b16),
-            pltpu.VMEM((2 * rows, antennas), b16),
+            pltpu.VMEM((3, antennas, 2 * rows), b16),
             pltpu.VMEM((2 * beams, antennas), f32),
             pltpu.VMEM((2 * beams, antennas), f32),
             pltpu.VMEM((2 * beams, antennas), f32),
@@ -440,7 +455,7 @@
         ),
     )(
         covariance.reshape(2 * rows, antennas),
-        start_columns,
+        start_columns.reshape(count, 1),
         rfi_flags.reshape(1, 1),
         steering,
     )

time: 362 us -> 346 us (0.956)
  Pallas kernels: 355 us -> 339 us
    pallas_call x1, Pallas kernels: 190 us -> 173 us  [beam_weights(): pl.pallas_call(functools.partial(tail_kernel, peers), out_shape=jax.Shape...]
where the time goes in v3:
time: 346 us
  Pallas kernels  339 us (98%)
  local copies, waits for them, and re-layouts  4.95 us (1%)
    pallas_call x1, Pallas kernels, beam_weights(): pl.pallas_call(functools.partial(tail_kernel, peers), out_shape=jax.Shape...  173 us
    pallas_call x1, Pallas kernels, channel_covariance(): pl.pallas_call(functools.partial(covariance_kernel, peers, groups), out_s...  165 us

profile of v3, /device:TPU:0, one launch (start us, length us, event | category | flops | bytes accessed | tf_op | source)
XLA Modules:
  0.0 345.9 jit_solution(11811222180312867736)
XLA Ops:
  1.3 0.7 copy.6.columns_ref
  2.0 1.0 fusion.7
  3.0 0.0 copy-start
  3.0 1.6 copy-done
  4.6 165.4 %shard_map.62.cov_ref = f32[512,2048]{1,0:T(8,128)S(1)} custom-call(bf16[4,2,256,512]{3,2,1,0:T(8,128)(2,1)S(1)} %copy-done), custom_call_target="tpu_custom_call" | custom-call | tf_op jit(solution)/shard_map/pallas_call | solution.py:229
  170.1 173.2 %shard_map.63 = f32[16,256]{1,0:T(8,128)S(1)} custom-call(f32[512,2048]{1,0:T(8,128)S(1)} %shard_map.62.cov_ref, s32[32,1]{1,0:T(8,128)S(1)} %copy.6.columns_ref, s32[1,1]{1,0:T(1,128)} %bitcast.12.flag_ref, f32[16,2048]{1,0:T(8,128)S(1)} %maximum_bitcast_fusion.steer_ref), custom_call_target="tpu_custom_call" | custom-call | tf_op jit(solution)/shard_map/pallas_call | solution.py:430
  343.3 0.6 copy.9
  343.9 2.0 copy.12
  (1 shorter events, 0.0 us)
Async XLA Ops:
  3.0 1.6 copy-start

commit v4 on v3

--- a/solution.py
+++ b/solution.py
@@ -310,6 +310,41 @@
             copy.wait_send()
             copy.wait_recv()
 
+    half = peers // 2
+    line, side = me // 2, lax.rem(me, 2)
+    partner = 2 * line + 1 - side
+
+    def hand_over(block, tile, landed, target, send_sem, recv_sem, index):
+        return pltpu.make_async_remote_copy(
+            src_ref=block.at[tile],
+            dst_ref=block.at[landed],
+            send_sem=send_sem.at[index],
+            recv_sem=recv_sem.at[index],
+            device_id={"tile": target},
+            device_id_type=MESH,
+        )
+
+    def along(k):
+        return 2 * lax.rem(line + k + half, half) + side
+
+    def send_staged(block, send_sem, recv_sem):
+        for k in range(1, half):
+            hand_over(block, me, me, along(k), send_sem, recv_sem, k).start()
+        hand_over(block, me, me, partner, send_sem, recv_sem, half).start()
+
+    def arrive_staged(block, send_sem, recv_sem):
+        for k in range(1, half):
+            source = along(-k)
+            hand_over(block, me, source, along(k), send_sem, recv_sem, k).wait_recv()
+            hand_over(block, source, source, partner, send_sem, recv_sem, half + k).start()
+        for k in range(half):
+            source = along(-k)
+            across = 2 * (source // 2) + 1 - side
+            hand_over(block, source, across, partner, send_sem, recv_sem, half + k).wait_recv()
+            hand_over(block, source, source, partner, send_sem, recv_sem, half + k).wait_send()
+        for k in range(1, half):
+            hand_over(block, me, me, along(k), send_sem, recv_sem, k).wait_send()
+
     def whole(block):
         return jnp.concatenate([block[j] for j in range(peers)], 1)
 
@@ -325,7 +360,7 @@
     ).astype(jnp.bfloat16)
     picked = dot16(hot, parts_ref[0]) + (dot16(hot, parts_ref[1]) + dot16(hot, parts_ref[2]))
     vectors[0, me] = jnp.concatenate([picked[:, :rows], picked[:, rows:]], 0)
-    send(vectors.at[0], vec_send.at[0], vec_recv.at[0])
+    send_staged(vectors.at[0], vec_send.at[0], vec_recv.at[0])
 
     square = cov_ref[0:rows, own]
     on_diagonal = lax.broadcasted_iota(jnp.int32, (rows, rows), 0) == lax.broadcasted_iota(
@@ -337,7 +372,7 @@
 
     def subspace_round(step, carry):
         now, later = lax.rem(step, 2), lax.rem(step + 1, 2)
-        arrive(vectors.at[now], vec_send.at[now], vec_recv.at[now])
+        arrive_staged(vectors.at[now], vec_send.at[now], vec_recv.at[now])
         block = whole(vectors.at[now])
         size = 2 * count
         high, middle, low = split_thirds(block)
@@ -348,7 +383,7 @@
         factor = inverse_factor(*hermitian_parts(dot_nt(block, block), count), count)
         factor_ref[...] = factor
         vectors[later, me] = dot_nn(factor, moved)
-        send(vectors.at[later], vec_send.at[later], vec_recv.at[later])
+        send_staged(vectors.at[later], vec_send.at[later], vec_recv.at[later])
         return carry
 
     lax.fori_loop(0, SUB_ITERS, subspace_round, 0)
@@ -356,7 +391,7 @@
     flag = flag_ref[...].astype(jnp.float32)
     basis = dot_nn(factor_ref[...], whole(vectors.at[last])) * flag
     basis_ref[...] = basis
-    arrive(vectors.at[after], vec_send.at[after], vec_recv.at[after])
+    arrive_staged(vectors.at[after], vec_send.at[after], vec_recv.at[after])
     image = whole(vectors.at[after]) * flag
     inner = embed(*hermitian_parts(dot_nt(image, basis), count))
     wide_ref[0 : 2 * count, :] = image - 0.5 * dot_nn(inner, basis)

time: 346 us -> 334 us (0.965)
  Pallas kernels: 339 us -> 326 us
    pallas_call x1, Pallas kernels: 173 us -> 161 us  [beam_weights(): pl.pallas_call(functools.partial(tail_kernel, peers), out_shape=jax.Shape...]
where the time goes in v4:
time: 334 us
  Pallas kernels  326 us (98%)
  local copies, waits for them, and re-layouts  4.95 us (1%)
    pallas_call x1, Pallas kernels, channel_covariance(): pl.pallas_call(functools.partial(covariance_kernel, peers, groups), out_s...  165 us
    pallas_call x1, Pallas kernels, beam_weights(): pl.pallas_call(functools.partial(tail_kernel, peers), out_shape=jax.Shape...  161 us

profile of v4, /device:TPU:0, one launch (start us, length us, event | category | flops | bytes accessed | tf_op | source)
XLA Modules:
  0.0 333.7 jit_solution(8668910345712054738)
XLA Ops:
  1.3 0.7 copy.6.columns_ref
  2.0 1.0 fusion.7
  3.0 0.0 copy-start
  3.0 1.6 copy-done
  4.6 165.4 %shard_map.62.cov_ref = f32[512,2048]{1,0:T(8,128)S(1)} custom-call(bf16[4,2,256,512]{3,2,1,0:T(8,128)(2,1)S(1)} %copy-done), custom_call_target="tpu_custom_call" | custom-call | tf_op jit(solution)/shard_map/pallas_call | solution.py:229
  170.1 161.0 %shard_map.63 = f32[16,256]{1,0:T(8,128)S(1)} custom-call(f32[512,2048]{1,0:T(8,128)S(1)} %shard_map.62.cov_ref, s32[32,1]{1,0:T(8,128)S(1)} %copy.6.columns_ref, s32[1,1]{1,0:T(1,128)} %bitcast.12.flag_ref, f32[16,2048]{1,0:T(8,128)S(1)} %maximum_bitcast_fusion.steer_ref), custom_call_target="tpu_custom_call" | custom-call | tf_op jit(solution)/shard_map/pallas_call | solution.py:465
  331.1 0.6 copy.9
  331.7 2.0 copy.12
  (1 shorter events, 0.0 us)
Async XLA Ops:
  3.0 1.6 copy-start

commit v5 on v4

--- a/solution.py
+++ b/solution.py
@@ -437,8 +437,8 @@
         top = dot16(jnp.concatenate([high, low], 0), parts_ref[0])
         product = top[: 2 * beams] + top[2 * beams :] + dot16(high, parts_ref[1])
         mapped[slot, me] = complex_rows(product, beams, rows)
-        send(mapped.at[slot], map_send.at[slot], map_recv.at[slot])
-        arrive(mapped.at[slot], map_send.at[slot], map_recv.at[slot])
+        send_staged(mapped.at[slot], map_send.at[slot], map_recv.at[slot])
+        arrive_staged(mapped.at[slot], map_send.at[slot], map_recv.at[slot])
         combined = whole(mapped.at[slot]) + load * direction
         alpha = norm / inner_product(direction, combined)
         alpha_rows = both(alpha)

time: 334 us -> 359 us (1.075)
  Pallas kernels: 326 us -> 351 us
    pallas_call x1, Pallas kernels: 161 us -> 186 us  [beam_weights(): pl.pallas_call(functools.partial(tail_kernel, peers), out_shape=jax.Shape...]
where the time goes in v5:
time: 359 us; the launch traced here: 358 us
  Pallas kernels  351 us (98%)
  local copies, waits for them, and re-layouts  4.95 us (1%)
    pallas_call x1, Pallas kernels, beam_weights(): pl.pallas_call(functools.partial(tail_kernel, peers), out_shape=jax.Shape...  186 us
    pallas_call x1, Pallas kernels, channel_covariance(): pl.pallas_call(functools.partial(covariance_kernel, peers, groups), out_s...  165 us

profile of v5, /device:TPU:0, one launch (start us, length us, event | category | flops | bytes accessed | tf_op | source)
XLA Modules:
  0.0 358.5 jit_solution(14979682748350689840)
XLA Ops:
  1.3 0.7 copy.6.columns_ref
  2.0 1.0 fusion.7
  3.0 0.0 copy-start
  3.0 1.6 copy-done
  4.6 165.4 %shard_map.62.cov_ref = f32[512,2048]{1,0:T(8,128)S(1)} custom-call(bf16[4,2,256,512]{3,2,1,0:T(8,128)(2,1)S(1)} %copy-done), custom_call_target="tpu_custom_call" | custom-call | tf_op jit(solution)/shard_map/pallas_call | solution.py:229
  170.1 185.8 %shard_map.63 = f32[16,256]{1,0:T(8,128)S(1)} custom-call(f32[512,2048]{1,0:T(8,128)S(1)} %shard_map.62.cov_ref, s32[32,1]{1,0:T(8,128)S(1)} %copy.6.columns_ref, s32[1,1]{1,0:T(1,128)} %bitcast.12.flag_ref, f32[16,2048]{1,0:T(8,128)S(1)} %maximum_bitcast_fusion.steer_ref), custom_call_target="tpu_custom_call" | custom-call | tf_op jit(solution)/shard_map/pallas_call | solution.py:465
  355.8 0.6 copy.9
  356.5 2.0 copy.12
  (1 shorter events, 0.0 us)
Async XLA Ops:
  3.0 1.6 copy-start
